TPU v7x, 128 devices: a whole 4x4x4 slice. The times are simulated.
128 devices in a mesh: bx: 8 (over y_hi, z), by: 16 (over y_lo, x, core).
Axes of the slice: x: 4, y: 4 (y_hi: 2, y_lo: 2; y = y_hi * 2 + y_lo), z: 4, core: 2. Of those that a mesh axis runs over, the one named last changes fastest.
Arguments:
- excitation: bfloat16 [64, 128, 32, 128], P('bx', 'by'), may hold values from -6 to 6
- area: bfloat16 [64, 128, 128], P('bx', 'by'), may hold values from 1 to 8
- conductor: int32 [64, 128, 128], P('bx', 'by'), may hold values from 0 to 31
- near_blocks: bfloat16 [64, 128, 9, 128, 128], P('bx', 'by'), may hold values from -0.1875 to 0.1875
- near_mask: int32 [64, 128, 9], P('bx', 'by'), may hold values 0 or 1
- source_moments: bfloat16 [64, 128, 128, 128], P('bx', 'by'), may hold values from -0.5 to 0.5
- target_eval: bfloat16 [64, 128, 128, 128], P('bx', 'by'), may hold values from -0.5 to 0.5
- translations: bfloat16 [40, 128, 128], replicated, may hold values from -0.109375 to 0.109375
- shift_up: bfloat16 [2, 2, 128, 128], replicated, may hold values from -0.25 to 0.25
Outputs:
- potential: bfloat16 [64, 128, 32, 128], P('bx', 'by')
- adjoint_out: bfloat16 [64, 128, 32, 128], P('bx', 'by')
All inputs are finite; a program needn't handle non-finite values. No bound on the sum of `near_mask` on one device may be relied on, other than what follows from the above.
Results may differ from a plain program's by a relative error of at most 0.01.
Values may be sent and summed in bfloat16 or wider, within the bound.
A program may use at most 256 MiB of HBM per device.

v0:
```python
import jax
import jax.numpy as jnp
from jax import lax
from jax.experimental import pallas as pl
from jax.experimental.pallas import tpu as pltpu
from jax.sharding import PartitionSpec as P

MESH = pl.DeviceIdType.MESH
F32 = jnp.float32
BF16 = jnp.bfloat16
DIRS = [(dx, dy) for dx in (-1, 0, 1) for dy in (-1, 0, 1) if (dx, dy) != (0, 0)]
NEAR = [(dx, dy) for dx in (-1, 0, 1) for dy in (-1, 0, 1)]
FAR = [(dx, dy) for dx in range(-3, 4) for dy in range(-3, 4) if max(abs(dx), abs(dy)) >= 2]
OFF1, OFF2, OFF3, OFF4, OFF5, ROWS = 512, 640, 672, 704, 736, 768


def nt(a, b):
    return lax.dot_general(a, b, (((1,), (1,)), ((), ())), preferred_element_type=F32)


def nn(a, b):
    return jnp.dot(a, b, preferred_element_type=F32)


def edge(step, size, width):
    if step == 0:
        return pl.ds(width, size), pl.ds(width, size)
    if step > 0:
        return pl.ds(size, width), pl.ds(0, width)
    return pl.ds(width, width), pl.ds(size + width, width)


def kernel(
    n_rows,
    n_cols,
    exc_hbm,
    area_hbm,
    cond_hbm,
    nb_hbm,
    mask_ref,
    sm_hbm,
    te_hbm,
    tr_hbm,
    su_hbm,
    pot_ref,
    adj_ref,
    epad,
    area_v,
    cond_v,
    nb_v,
    sm_v,
    te_v,
    tr_v,
    su_v,
    wts,
    leaf,
    l1,
    l2,
    l3,
    l4,
    l5,
    nf,
    acc,
    ret_row,
    ret_col,
    ret_cor,
    in_row,
    in_col,
    in_cor,
    wt,
    gain,
    sel5,
    sel4,
    sel3,
    loc2,
    loc1,
    locl,
    in_sem,
    map_sem,
    nb_sem,
    hs_sem,
    hr_sem,
    s3_sem,
    r3_sem,
    s3c_sem,
    r3c_sem,
    s4_sem,
    r4_sem,
):
    r = lax.axis_index("bx")
    c = lax.axis_index("by")
    r2, c2 = r // 2, c // 2
    r4, c4 = r // 4, c // 4

    cp_exc = pltpu.make_async_copy(exc_hbm, epad.at[1:9, 1:9], in_sem.at[0])
    cp_area = pltpu.make_async_copy(area_hbm, area_v, in_sem.at[1])
    cp_cond = pltpu.make_async_copy(cond_hbm, cond_v, in_sem.at[2])
    cp_su = pltpu.make_async_copy(su_hbm, su_v, in_sem.at[3])
    cp_tr = pltpu.make_async_copy(tr_hbm, tr_v, in_sem.at[4])

    def cp_sm(x):
        return pltpu.make_async_copy(sm_hbm.at[x], sm_v.at[x], map_sem.at[0, x])

    def cp_te(x):
        return pltpu.make_async_copy(te_hbm.at[x], te_v.at[x], map_sem.at[1, x])

    def cp_nb(x):
        return pltpu.make_async_copy(nb_hbm.at[x], nb_v.at[x], nb_sem.at[x])

    cp_exc.start()
    cp_area.start()
    cp_cond.start()
    for x in range(8):
        cp_sm(x).start()
        cp_te(x).start()
    cp_su.start()
    for x in range(8):
        cp_nb(x).start()
    cp_tr.start()

    def clear(ref, rows, cols, width, wide):
        ref[0:width] = jnp.zeros((width,) + ref.shape[1:], ref.dtype)
        ref[rows + width :] = jnp.zeros((width,) + ref.shape[1:], ref.dtype)
        side = jnp.zeros((rows, wide) + ref.shape[2:], ref.dtype)
        ref[width : rows + width, 0:wide] = side
        ref[width : rows + width, cols + wide :] = side

    clear(epad, 8, 8, 1, 1)
    clear(leaf, 8, 4, 2, 1)
    clear(l1, 4, 2, 2, 1)
    clear(l2, 2, 1, 2, 1)
    for ref in (l3, l4, l5, in_row, in_col, in_cor, acc):
        ref[...] = jnp.zeros(ref.shape, ref.dtype)

    def inside(row, col):
        return (row >= 0) & (row < n_rows) & (col >= 0) & (col < n_cols)

    def row_peers():
        return [(row, row != r) for row in range(n_rows)]

    def col_peers():
        base = 2 * c2 - 2
        return [
            (j, base + j, (base + j != c) & (base + j >= 0) & (base + j < n_cols)) for j in range(6)
        ]

    def pair_peers():
        return [(v, 2 * v + c % 2, v != c2) for v in range(n_cols // 2)]

    barrier = pltpu.get_barrier_semaphore()
    greeted = jnp.int32(0)

    def greet(row, col, present):
        @pl.when(present)
        def _():
            pl.semaphore_signal(barrier, inc=1, device_id=(row, col), device_id_type=MESH)

        return present.astype(jnp.int32)

    for dx, dy in DIRS:
        greeted = greeted + greet(r + dx, c + dy, inside(r + dx, c + dy))
    for row, present in row_peers():
        greeted = greeted + greet(jnp.int32(row), c, present)
    for _, col, present in col_peers():
        greeted = greeted + greet(r, col, present)
    for _, col, present in pair_peers():
        greeted = greeted + greet(r, col, present)
    pl.semaphore_wait(barrier, greeted)

    def message(number, direction):
        dx, dy = DIRS[direction]
        if number == 4:
            if dy == 0:
                place = 0 if dx > 0 else 1
                return ret_row.at[place], in_row.at[place]
            if dx == 0:
                place = 0 if dy > 0 else 1
                return ret_col.at[place], in_col.at[place]
            place = (0 if dx > 0 else 2) + (0 if dy > 0 else 1)
            return ret_cor.at[place], in_cor.at[place]
        ref, rows, width, cols, wide = (
            (epad, 8, 1, 8, 1),
            (leaf, 8, 2, 4, 1),
            (l1, 4, 2, 2, 1),
            (l2, 2, 2, 1, 1),
        )[number]
        src_rows, dst_rows = edge(dx, rows, width)
        src_cols, dst_cols = edge(dy, cols, wide)
        return ref.at[src_rows, src_cols], ref.at[dst_rows, dst_cols]

    def halo_copy(number, direction):
        dx, dy = DIRS[direction]
        src, dst = message(number, direction)
        return pltpu.make_async_remote_copy(
            src_ref=src,
            dst_ref=dst,
            send_sem=hs_sem.at[number, direction],
            recv_sem=hr_sem.at[number, direction],
            device_id=(r + dx, c + dy),
            device_id_type=MESH,
        )

    def halo_start(number):
        for direction, (dx, dy) in enumerate(DIRS):

            @pl.when(inside(r + dx, c + dy))
            def _():
                halo_copy(number, direction).start()

    def halo_received(number):
        for direction, (dx, dy) in enumerate(DIRS):

            @pl.when(inside(r - dx, c - dy))
            def _():
                halo_copy(number, direction).wait_recv()

    def halo_sent(number):
        for direction, (dx, dy) in enumerate(DIRS):

            @pl.when(inside(r + dx, c + dy))
            def _():
                halo_copy(number, direction).wait_send()

    def l3_row_copy(row, sender):
        return pltpu.make_async_remote_copy(
            src_ref=l3.at[2 + c % 2, sender + 2],
            dst_ref=l3.at[2 + c % 2, sender + 2],
            send_sem=s3_sem.at[row],
            recv_sem=r3_sem.at[sender],
            device_id=(jnp.int32(row), c),
            device_id_type=MESH,
        )

    def l3_col_copy(j, col):
        return pltpu.make_async_remote_copy(
            src_ref=l3.at[2 + c % 2],
            dst_ref=l3.at[c - (2 * (col // 2) - 2)],
            send_sem=s3c_sem.at[j],
            recv_sem=r3c_sem.at[c - (2 * (col // 2) - 2)],
            device_id=(r, col),
            device_id_type=MESH,
        )

    def l3_col_wait(j, col):
        return pltpu.make_async_remote_copy(
            src_ref=l3.at[2 + c % 2],
            dst_ref=l3.at[j],
            send_sem=s3c_sem.at[j],
            recv_sem=r3c_sem.at[j],
            device_id=(r, col),
            device_id_type=MESH,
        )

    def l4_copy(v, col, owner):
        return pltpu.make_async_remote_copy(
            src_ref=l4.at[owner + 2, pl.ds(2, n_rows // 2)],
            dst_ref=l4.at[owner + 2, pl.ds(2, n_rows // 2)],
            send_sem=s4_sem.at[v],
            recv_sem=r4_sem.at[owner],
            device_id=(r, col),
            device_id_type=MESH,
        )

    cp_exc.wait()
    halo_start(0)
    cp_area.wait()
    cp_cond.wait()

    labels = lax.broadcasted_iota(jnp.int32, (32, 128), 0)

    def moments(x, carry):
        cp_sm(x).wait()
        cp_te(x).wait()
        conds = cond_v[x]
        areas = area_v[x].astype(F32)
        for y in range(8):
            half = slice((y % 2) * 128, (y % 2) * 128 + 128)
            chosen = labels == conds[y : y + 1]
            w = jnp.where(chosen, areas[y : y + 1], 0.0).astype(BF16)
            wts[x, y] = w
            leaf[x + 2, 1 + y // 2, 0, :, half] = nt(epad[x + 1, y + 1], sm_v[x, y]).astype(BF16)
            leaf[x + 2, 1 + y // 2, 1, :, half] = nn(w, te_v[x, y]).astype(BF16)
        return carry

    lax.fori_loop(0, 8, moments, 0)

    cp_su.wait()
    ups = [jnp.concatenate([su_v[a, 0], su_v[a, 1]], axis=1) for a in range(2)]

    for u in range(4):
        total = sum(nt(leaf[2 * u + a + 2, 1:5].reshape(256, 256), ups[a]) for a in range(2))
        made = total.astype(BF16).reshape(4, 2, 32, 128)
        for v in range(4):
            l1[u + 2, 1 + v // 2, :, :, (v % 2) * 128 : (v % 2) * 128 + 128] = made[v]
    total = sum(
        nt(jnp.concatenate([l1[2 * u + a + 2, 1:3].reshape(128, 256) for u in range(2)]), ups[a])
        for a in range(2)
    )
    made = total.astype(BF16).reshape(2, 2, 2, 32, 128)
    for u in range(2):
        for v in range(2):
            l2[u + 2, 1, :, :, v * 128 : v * 128 + 128] = made[u, v]
    total = sum(nt(l2[a + 2, 1].reshape(64, 256), ups[a]) for a in range(2))
    l3[2 + c % 2, r + 2] = total.astype(BF16).reshape(2, 32, 128)

    for row, present in row_peers():

        @pl.when(present)
        def _():
            l3_row_copy(row, r).start()

    halo_start(3)
    halo_start(2)
    halo_start(1)

    halo_received(0)

    def near(x, carry):
        cp_nb(x).wait()
        for y in range(8):
            blocks = jnp.concatenate([nb_v[x, y, k] for k in range(9)], axis=1)
            keep = [mask_ref[x, y, k].astype(F32) for k in range(9)]
            source = jnp.concatenate(
                [
                    (epad[x + 1 + dx, y + 1 + dy].astype(F32) * keep[k]).astype(BF16)
                    for k, (dx, dy) in enumerate(NEAR)
                ],
                axis=1,
            )
            nf[x, y] = nt(source, blocks)
            back = nn(wts[x, y], blocks)
            for k, (dx, dy) in enumerate(NEAR):
                acc[x + 1 + dx, y + 1 + dy] += keep[k] * back[:, k * 128 : k * 128 + 128]
        return carry

    lax.fori_loop(0, 2, near, 0)

    for row, present in row_peers():

        @pl.when(present)
        def _():
            l3_row_copy(row, jnp.int32(row)).wait_recv()

    for j, col, present in col_peers():

        @pl.when(present)
        def _():
            l3_col_copy(j, col).start()

    lax.fori_loop(2, 4, near, 0)

    for j, col, present in col_peers():

        @pl.when(present)
        def _():
            l3_col_wait(j, col).wait_recv()

    def up_strip(ref, col, rows):
        total = 0.0
        for a in range(2):
            pairs = [
                jnp.concatenate(
                    [
                        ref[col, 2 * u + a + 2].reshape(64, 128),
                        ref[col + 1, 2 * u + a + 2].reshape(64, 128),
                    ],
                    axis=1,
                )
                for u in range(rows)
            ]
            total = total + nt(jnp.concatenate(pairs, axis=0), ups[a])
        return total.astype(BF16).reshape(rows, 2, 32, 128)

    l4[c2 + 2, 2 : 2 + n_rows // 2] = up_strip(l3, 2, n_rows // 2)
    for v, col, present in pair_peers():

        @pl.when(present)
        def _():
            l4_copy(v, col, c2).start()

    lax.fori_loop(4, 6, near, 0)

    for v, col, present in pair_peers():

        @pl.when(present)
        def _():
            l4_copy(v, col, jnp.int32(v)).wait_recv()

    for col in range(n_cols // 4):
        l5[col + 2, 2 : 2 + n_rows // 4] = up_strip(l4, 2 + 2 * col, n_rows // 4)

    lax.fori_loop(6, 8, near, 0)

    for place, row in ((0, 9), (1, 0)):
        ret_row[place] = acc[row, 1:9].astype(BF16)
        ret_col[place] = acc[1:9, row].astype(BF16)
        for other, col in ((0, 9), (1, 0)):
            ret_cor[2 * place + other] = acc[row, col].astype(BF16)
    halo_start(4)

    cp_tr.wait()
    for dx in range(-3, 4):
        for dy in range(-1, 2):
            for i in range(2):
                for j in range(2):
                    offset = (dx, 2 * dy + j - i)
                    block = (
                        tr_v[FAR.index(offset)] if offset in FAR else jnp.zeros((128, 128), BF16)
                    )
                    wt[
                        3 * (dx + 3) + dy + 1,
                        i * 128 : i * 128 + 128,
                        j * 128 : j * 128 + 128,
                    ] = block

    halo_received(3)
    halo_received(2)
    halo_received(1)

    def sources(side, a, dx, dy):
        parts = []
        for i in range(4):
            parts.append(leaf[2 * i + a + dx + 2, 1 + dy : 5 + dy, side].reshape(128, 256))
        for i in range(2):
            parts.append(l1[2 * i + a + dx + 2, 1 + dy : 3 + dy, side].reshape(64, 256))
        parts.append(l2[a + dx + 2, 1 + dy, side])
        for ref, row, col in (
            (l3, 2 * r2, 0),
            (l4, 2 * r4, 2 * c4),
            (l5, 0, 2 * (c // 8)),
        ):
            row = row + a + dx + 2
            col = col + 2 * (1 + dy)
            parts.append(jnp.concatenate([ref[col, row, side], ref[col + 1, row, side]], axis=1))
        return jnp.concatenate(parts, axis=0)

    def interact(side, a, dx, columns):
        taken = jnp.concatenate([sources(side, a, dx, dy) for dy in columns], axis=1)
        if side == 0:
            tiles = [wt[3 * (dx + 3) + dy + 1] for dy in columns]
            return nt(taken, jnp.concatenate(tiles, axis=1))
        tiles = [wt[3 * (3 - dx) + 1 - dy] for dy in columns]
        return nn(taken, jnp.concatenate(tiles, axis=0))

    for side in range(2):
        for a in range(2):
            gain[side, a] = jnp.zeros((ROWS, 256), F32)

            def outer(i, carry):
                dx = i - 3 + 3 * (i // 2) if a == 1 else i + 1 - 3 * ((2 - i) // 2)
                gain[side, a] += interact(side, a, dx, (-1, 0, 1))
                return carry

            def inner(i, carry):
                gain[side, a] += interact(side, a, i - 1, (-1, 1))
                return carry

            lax.fori_loop(0, 3, outer, 0)
            lax.fori_loop(0, 3, inner, 0)

    for a in range(2):
        for side in range(2):
            top = gain[side, a, OFF5 : OFF5 + 32].astype(BF16)
            for b in range(2):
                sel5[a, b, side] = top[:, b * 128 : b * 128 + 128]
    parent = sel5[r4, c4 % 2].reshape(64, 128)
    for off, sel, row, col in (
        (OFF4, sel4, r2 % 2, c2 % 2),
        (OFF3, sel3, r % 2, c % 2),
        (OFF2, loc2, None, None),
    ):
        for a in range(2):
            spread = nn(parent, ups[a])
            for side in range(2):
                made = spread[side * 32 : side * 32 + 32] + gain[side, a, off : off + 32]
                made = made.astype(BF16)
                for b in range(2):
                    sel[a, b, side] = made[:, b * 128 : b * 128 + 128]
        if row is not None:
            parent = sel[row, col].reshape(64, 128)

    for upper, lower, count, off in ((loc2, loc1, 2, OFF1), (loc1, locl, 4, 0)):
        for u in range(count):
            for a in range(2):
                spread = nn(upper[u].reshape(count * 64, 128), ups[a])
                for v in range(count):
                    for side in range(2):
                        first = v * 64 + side * 32
                        at = off + (u * count + v) * 32
                        made = spread[first : first + 32] + gain[side, a, at : at + 32]
                        made = made.astype(BF16)
                        for b in range(2):
                            lower[2 * u + a, 2 * v + b, side] = made[:, b * 128 : b * 128 + 128]

    halo_received(4)
    for place, row in ((0, 1), (1, 8)):
        acc[row, 1:9] += in_row[place].astype(F32)
        acc[1:9, row] += in_col[place].astype(F32)
        for other, col in ((0, 1), (1, 8)):
            acc[row, col] += in_cor[2 * place + other].astype(F32)

    def finish(x, carry):
        for y in range(8):
            pot_ref[x, y] = (nf[x, y] + nt(locl[x, y, 0], te_v[x, y])).astype(BF16)
            adj_ref[x, y] = (acc[x + 1, y + 1] + nn(locl[x, y, 1], sm_v[x, y])).astype(BF16)
        return carry

    lax.fori_loop(0, 8, finish, 0)

    for number in range(5):
        halo_sent(number)
    for row, present in row_peers():

        @pl.when(present)
        def _():
            l3_row_copy(row, r).wait_send()

    for j, col, present in col_peers():

        @pl.when(present)
        def _():
            l3_col_copy(j, col).wait_send()

    for v, col, present in pair_peers():

        @pl.when(present)
        def _():
            l4_copy(v, col, c2).wait_send()


def solution(mesh):
    n_rows, n_cols = mesh.shape["bx"], mesh.shape["by"]
    hbm = pl.BlockSpec(memory_space=pl.ANY)
    vmem = pl.BlockSpec(memory_space=pltpu.VMEM)
    smem = pl.BlockSpec(memory_space=pltpu.SMEM)
    box = (2, 32, 128)
    pair = (2, 32, 256)
    scratch = [
        pltpu.VMEM((10, 10, 32, 128), BF16),
        pltpu.VMEM((8, 8, 128), BF16),
        pltpu.VMEM((8, 8, 128), jnp.int32),
        pltpu.VMEM((8, 8, 9, 128, 128), BF16),
        pltpu.VMEM((8, 8, 128, 128), BF16),
        pltpu.VMEM((8, 8, 128, 128), BF16),
        pltpu.VMEM((40, 128, 128), BF16),
        pltpu.VMEM((2, 2, 128, 128), BF16),
        pltpu.VMEM((8, 8, 32, 128), BF16),
        pltpu.VMEM((12, 6) + pair, BF16),
        pltpu.VMEM((8, 4) + pair, BF16),
        pltpu.VMEM((6, 3) + pair, BF16),
        pltpu.VMEM((6, n_rows + 4) + box, BF16),
        pltpu.VMEM((n_cols // 2 + 4, n_rows // 2 + 4) + box, BF16),
        pltpu.VMEM((n_cols // 4 + 4, n_rows // 4 + 4) + box, BF16),
        pltpu.VMEM((8, 8, 32, 128), F32),
        pltpu.VMEM((10, 10, 32, 128), F32),
        pltpu.VMEM((2, 8, 32, 128), BF16),
        pltpu.VMEM((2, 8, 32, 128), BF16),
        pltpu.VMEM((4, 32, 128), BF16),
        pltpu.VMEM((2, 8, 32, 128), BF16),
        pltpu.VMEM((2, 8, 32, 128), BF16),
        pltpu.VMEM((4, 32, 128), BF16),
        pltpu.VMEM((21, 256, 256), BF16),
        pltpu.VMEM((2, 2, ROWS, 256), F32),
        pltpu.VMEM((2, 2) + box, BF16),
        pltpu.VMEM((2, 2) + box, BF16),
        pltpu.VMEM((2, 2) + box, BF16),
        pltpu.VMEM((2, 2) + box, BF16),
        pltpu.VMEM((4, 4) + box, BF16),
        pltpu.VMEM((8, 8) + box, BF16),
        pltpu.SemaphoreType.DMA((5,)),
        pltpu.SemaphoreType.DMA((2, 8)),
        pltpu.SemaphoreType.DMA((8,)),
        pltpu.SemaphoreType.DMA((5, 8)),
        pltpu.SemaphoreType.DMA((5, 8)),
        pltpu.SemaphoreType.DMA((n_rows,)),
        pltpu.SemaphoreType.DMA((n_rows,)),
        pltpu.SemaphoreType.DMA((6,)),
        pltpu.SemaphoreType.DMA((6,)),
        pltpu.SemaphoreType.DMA((n_cols // 2,)),
        pltpu.SemaphoreType.DMA((n_cols // 2,)),
    ]

    def per_device(*arrays):
        def body(*refs):
            kernel(n_rows, n_cols, *refs)

        result = jax.ShapeDtypeStruct(arrays[0].shape, BF16)
        return pl.pallas_call(
            body,
            out_shape=(result, result),
            in_specs=[hbm, hbm, hbm, hbm, smem, hbm, hbm, hbm, hbm],
            out_specs=(vmem, vmem),
            scratch_shapes=scratch,
            compiler_params=pltpu.CompilerParams(
                collective_id=0, has_side_effects=True, vmem_limit_bytes=56 * 1024 * 1024
            ),
            cost_estimate=pl.CostEstimate(
                flops=4300000000, bytes_accessed=26000000, transcendentals=0
            ),
            name="fmm",
        )(*arrays)

    placed = (
        P("bx", "by", None, None),
        P("bx", "by", None),
        P("bx", "by", None),
        P("bx", "by", None, None, None),
        P("bx", "by", None),
        P("bx", "by", None, None),
        P("bx", "by", None, None),
        P(),
        P(),
    )
    return jax.shard_map(
        per_device,
        mesh=mesh,
        in_specs=placed,
        out_specs=(P("bx", "by", None, None), P("bx", "by", None, None)),
        check_vma=False,
    )
```

profile of v0, /device:TPU:22, one launch (start us, length us, event | category | flops | bytes accessed | tf_op | source)
XLA Modules:
  0.0 75.7 jit_solution(16095092350898748965)
XLA Ops:
  0.6 71.3 %fmm.1 = (bf16[8,8,32,128]{3,2,1,0:T(8,128)(2,1)}, bf16[8,8,32,128]{3,2,1,0:T(8,128)(2,1)}) custom-call(bf16[8,8,32,128]{3,2,1,0:T(8,128)(2,1)} %refs_0_.1, bf16[8,8,128]{2,1,0:T(8,128)(2,1)} %refs_1_.1, s32[8,8,128]{2,1,0:T(8,128)} %refs_2_.1, bf16[8,8,9,128,128]{4,3,2,1,0:T(8,128)(2,1)} %refs_3_.1, s32[8,8,9]{2,1,0:T(8,128)} %refs_4_.1, ...), custom_call_target="tpu_custom_call" | custom-call | flops 4300000256 | bytes 26000000 | tf_op jit(solution)/shard_map/fmm/pallas_call | solution.py:588
  72.0 1.9 %copy.13 = bf16[8,8,32,128]{3,2,1,0:T(8,128)(2,1)} copy(bf16[8,8,32,128]{3,2,1,0:T(8,128)(2,1)} %get-tuple-element.4) | data formatting | bytes 1048576
  73.8 1.9 %copy.14 = bf16[8,8,32,128]{3,2,1,0:T(8,128)(2,1)} copy(bf16[8,8,32,128]{3,2,1,0:T(8,128)(2,1)} %get-tuple-element.5) | data formatting | bytes 1048576
where the time goes:
time: 76 us; the launch traced here: 75.7 us
  Pallas kernels  71.3 us (94%)
  local copies, waits for them, and re-layouts  3.74 us (5%)
    pallas_call x1, Pallas kernels, per_device(): pl.pallas_call(body, out_shape=(result, result), in_specs=[hbm, hbm, hbm,...  71.3 us
    unnamed x2, local copies, waits for them, and re-layouts  3.74 us

commit v1 on v0

--- a/solution.py
+++ b/solution.py
@@ -63,10 +63,8 @@
     acc,
     ret_row,
     ret_col,
-    ret_cor,
     in_row,
     in_col,
-    in_cor,
     wt,
     gain,
     sel5,
@@ -82,8 +80,8 @@
     hr_sem,
     s3_sem,
     r3_sem,
-    s3c_sem,
-    r3c_sem,
+    sp_sem,
+    rp_sem,
     s4_sem,
     r4_sem,
 ):
@@ -129,7 +127,7 @@
     clear(leaf, 8, 4, 2, 1)
     clear(l1, 4, 2, 2, 1)
     clear(l2, 2, 1, 2, 1)
-    for ref in (l3, l4, l5, in_row, in_col, in_cor, acc):
+    for ref in (l3, l4, l5, in_row, in_col):
         ref[...] = jnp.zeros(ref.shape, ref.dtype)
 
     def inside(row, col):
@@ -138,12 +136,6 @@
     def row_peers():
         return [(row, row != r) for row in range(n_rows)]
 
-    def col_peers():
-        base = 2 * c2 - 2
-        return [
-            (j, base + j, (base + j != c) & (base + j >= 0) & (base + j < n_cols)) for j in range(6)
-        ]
-
     def pair_peers():
         return [(v, 2 * v + c % 2, v != c2) for v in range(n_cols // 2)]
 
@@ -157,67 +149,69 @@
 
         return present.astype(jnp.int32)
 
-    for dx, dy in DIRS:
-        greeted = greeted + greet(r + dx, c + dy, inside(r + dx, c + dy))
+    for dy in (-1, 1):
+        greeted = greeted + greet(r, c + dy, inside(r, c + dy))
     for row, present in row_peers():
         greeted = greeted + greet(jnp.int32(row), c, present)
-    for _, col, present in col_peers():
-        greeted = greeted + greet(r, col, present)
     for _, col, present in pair_peers():
         greeted = greeted + greet(r, col, present)
     pl.semaphore_wait(barrier, greeted)
 
-    def message(number, direction):
+    def halo_copy(number, direction):
         dx, dy = DIRS[direction]
         if number == 4:
-            if dy == 0:
-                place = 0 if dx > 0 else 1
-                return ret_row.at[place], in_row.at[place]
-            if dx == 0:
-                place = 0 if dy > 0 else 1
-                return ret_col.at[place], in_col.at[place]
-            place = (0 if dx > 0 else 2) + (0 if dy > 0 else 1)
-            return ret_cor.at[place], in_cor.at[place]
-        ref, rows, width, cols, wide = (
-            (epad, 8, 1, 8, 1),
-            (leaf, 8, 2, 4, 1),
-            (l1, 4, 2, 2, 1),
-            (l2, 2, 2, 1, 1),
-        )[number]
-        src_rows, dst_rows = edge(dx, rows, width)
-        src_cols, dst_cols = edge(dy, cols, wide)
-        return ref.at[src_rows, src_cols], ref.at[dst_rows, dst_cols]
-
-    def halo_copy(number, direction):
-        dx, dy = DIRS[direction]
-        src, dst = message(number, direction)
+            place = 0 if dx + dy > 0 else 1
+            src, dst = (ret_row, in_row) if dy == 0 else (ret_col, in_col)
+            src, dst = src.at[place], dst.at[place]
+        else:
+            ref, rows, width, cols, wide = (
+                (epad, 8, 1, 8, 1),
+                (leaf, 8, 2, 4, 1),
+                (l1, 4, 2, 2, 1),
+                (l2, 2, 2, 1, 1),
+            )[number]
+            src_rows, dst_rows = edge(dx, rows, width)
+            src_cols, dst_cols = edge(dy, cols, wide)
+            src = ref.at[src_rows if dy == 0 or dx == 0 else dst_rows, src_cols]
+            dst = ref.at[dst_rows, dst_cols]
         return pltpu.make_async_remote_copy(
             src_ref=src,
             dst_ref=dst,
             send_sem=hs_sem.at[number, direction],
             recv_sem=hr_sem.at[number, direction],
-            device_id=(r + dx, c + dy),
+            device_id=(r + dx, c) if dy == 0 else (r, c + dy),
             device_id_type=MESH,
         )
 
-    def halo_start(number):
-        for direction, (dx, dy) in enumerate(DIRS):
-
-            @pl.when(inside(r + dx, c + dy))
+    ROW = [i for i, (dx, dy) in enumerate(DIRS) if dy == 0]
+    COL = [i for i, (dx, dy) in enumerate(DIRS) if dx == 0]
+    CORNER = [i for i, (dx, dy) in enumerate(DIRS) if dx * dy != 0]
+
+    def leaves(direction):
+        dx, dy = DIRS[direction]
+        if dy == 0:
+            return inside(r + dx, c)
+        return inside(r - dx, c) & inside(r, c + dy)
+
+    def halo_start(number, directions):
+        for direction in directions:
+
+            @pl.when(leaves(direction))
             def _():
                 halo_copy(number, direction).start()
 
-    def halo_received(number):
-        for direction, (dx, dy) in enumerate(DIRS):
+    def halo_received(number, directions):
+        for direction in directions:
+            dx, dy = DIRS[direction]
 
             @pl.when(inside(r - dx, c - dy))
             def _():
                 halo_copy(number, direction).wait_recv()
 
-    def halo_sent(number):
-        for direction, (dx, dy) in enumerate(DIRS):
-
-            @pl.when(inside(r + dx, c + dy))
+    def halo_sent(number, directions):
+        for direction in directions:
+
+            @pl.when(leaves(direction))
             def _():
                 halo_copy(number, direction).wait_send()
 
@@ -231,38 +225,72 @@
             device_id_type=MESH,
         )
 
-    def l3_col_copy(j, col):
+    other = c + 1 - 2 * (c % 2)
+
+    def l3_col_copy(step, received=False):
+        rows = pl.ds(2, n_rows) if step == 0 else pl.ds(2 * r2, 6)
+        own = 2 + c % 2
+        there = 2 + (1 - c % 2) if received else own
+        if step == 0:
+            src, dst, col = own, there, other
+        elif step == 1:
+            src, dst, col = own, c % 2, c + 2
+        elif step == 2:
+            src, dst, col = own, 4 + c % 2, c - 2
+        else:
+            src = c % 2 + (0 if step == 3 else 4)
+            dst = (1 - c % 2 if received else c % 2) + (0 if step == 3 else 4)
+            col = other
         return pltpu.make_async_remote_copy(
-            src_ref=l3.at[2 + c % 2],
-            dst_ref=l3.at[c - (2 * (col // 2) - 2)],
-            send_sem=s3c_sem.at[j],
-            recv_sem=r3c_sem.at[c - (2 * (col // 2) - 2)],
+            src_ref=l3.at[src, rows],
+            dst_ref=l3.at[dst, rows],
+            send_sem=sp_sem.at[step],
+            recv_sem=rp_sem.at[step],
             device_id=(r, col),
             device_id_type=MESH,
         )
 
-    def l3_col_wait(j, col):
+    has_last, has_next = c2 > 0, c2 < n_cols // 2 - 1
+    COL_SENDS = (True, has_next, has_last, has_last, has_next)
+    COL_COMES = (True, has_last, has_next, has_last, has_next)
+
+    part = n_rows // 4
+
+    def l4_copy(v, col, owner):
+        rows = pl.ds(2 + part * (c % 2), part)
         return pltpu.make_async_remote_copy(
-            src_ref=l3.at[2 + c % 2],
-            dst_ref=l3.at[j],
-            send_sem=s3c_sem.at[j],
-            recv_sem=r3c_sem.at[j],
-            device_id=(r, col),
-            device_id_type=MESH,
-        )
-
-    def l4_copy(v, col, owner):
-        return pltpu.make_async_remote_copy(
-            src_ref=l4.at[owner + 2, pl.ds(2, n_rows // 2)],
-            dst_ref=l4.at[owner + 2, pl.ds(2, n_rows // 2)],
+            src_ref=l4.at[owner + 2, rows],
+            dst_ref=l4.at[owner + 2, rows],
             send_sem=s4_sem.at[v],
             recv_sem=r4_sem.at[owner],
             device_id=(r, col),
             device_id_type=MESH,
         )
 
+    def l4_pass(half):
+        place = l4.at[pl.ds(2, n_cols // 2), pl.ds(2 + part * half, part)]
+        return pltpu.make_async_remote_copy(
+            src_ref=place,
+            dst_ref=place,
+            send_sem=sp_sem.at[5],
+            recv_sem=rp_sem.at[5],
+            device_id=(r, other),
+            device_id_type=MESH,
+        )
+
+    def l3_col_start(step):
+        @pl.when(COL_SENDS[step])
+        def _():
+            l3_col_copy(step).start()
+
+    def l3_col_received(step):
+        @pl.when(COL_COMES[step])
+        def _():
+            l3_col_copy(step, True).wait_recv()
+
     cp_exc.wait()
-    halo_start(0)
+    halo_start(0, ROW + COL)
+    acc[...] = jnp.zeros(acc.shape, F32)
     cp_area.wait()
     cp_cond.wait()
 
@@ -309,11 +337,27 @@
         def _():
             l3_row_copy(row, r).start()
 
-    halo_start(3)
-    halo_start(2)
-    halo_start(1)
-
-    halo_received(0)
+    halo_received(0, ROW)
+    halo_start(0, CORNER)
+    for number in (3, 2, 1):
+        halo_start(number, ROW + COL)
+
+    cp_tr.wait()
+    for dx in range(-3, 4):
+        for dy in range(-1, 2):
+            for i in range(2):
+                for j in range(2):
+                    offset = (dx, 2 * dy + j - i)
+                    block = (
+                        tr_v[FAR.index(offset)] if offset in FAR else jnp.zeros((128, 128), BF16)
+                    )
+                    wt[
+                        3 * (dx + 3) + dy + 1,
+                        i * 128 : i * 128 + 128,
+                        j * 128 : j * 128 + 128,
+                    ] = block
+
+    halo_received(0, COL + CORNER)
 
     def near(x, carry):
         cp_nb(x).wait()
@@ -341,28 +385,23 @@
         def _():
             l3_row_copy(row, jnp.int32(row)).wait_recv()
 
-    for j, col, present in col_peers():
-
-        @pl.when(present)
-        def _():
-            l3_col_copy(j, col).start()
+    for step in range(3):
+        l3_col_start(step)
+    halo_received(3, ROW)
+    halo_start(3, CORNER)
 
     lax.fori_loop(2, 4, near, 0)
 
-    for j, col, present in col_peers():
-
-        @pl.when(present)
-        def _():
-            l3_col_wait(j, col).wait_recv()
-
-    def up_strip(ref, col, rows):
+    l3_col_received(0)
+
+    def up_strip(ref, col, first, rows):
         total = 0.0
         for a in range(2):
             pairs = [
                 jnp.concatenate(
                     [
-                        ref[col, 2 * u + a + 2].reshape(64, 128),
-                        ref[col + 1, 2 * u + a + 2].reshape(64, 128),
+                        ref[col, first + 2 * u + a].reshape(64, 128),
+                        ref[col + 1, first + 2 * u + a].reshape(64, 128),
                     ],
                     axis=1,
                 )
@@ -371,51 +410,46 @@
             total = total + nt(jnp.concatenate(pairs, axis=0), ups[a])
         return total.astype(BF16).reshape(rows, 2, 32, 128)
 
-    l4[c2 + 2, 2 : 2 + n_rows // 2] = up_strip(l3, 2, n_rows // 2)
+    l4[c2 + 2, pl.ds(2 + part * (c % 2), part)] = up_strip(l3, 2, 2 + 2 * part * (c % 2), part)
     for v, col, present in pair_peers():
 
         @pl.when(present)
         def _():
             l4_copy(v, col, c2).start()
 
+    l3_col_received(1)
+    l3_col_start(3)
+    l3_col_received(2)
+    l3_col_start(4)
+    halo_received(2, ROW)
+    halo_start(2, CORNER)
+
     lax.fori_loop(4, 6, near, 0)
 
+    halo_received(1, ROW)
+    halo_start(1, CORNER)
     for v, col, present in pair_peers():
 
         @pl.when(present)
         def _():
             l4_copy(v, col, jnp.int32(v)).wait_recv()
 
+    l4_pass(c % 2).start()
+
+    lax.fori_loop(6, 8, near, 0)
+
+    for place, row in ((0, 9), (1, 0)):
+        ret_row[place] = acc[row].astype(BF16)
+    halo_start(4, ROW)
+
+    l3_col_received(3)
+    l3_col_received(4)
+    l4_pass(1 - c % 2).wait_recv()
     for col in range(n_cols // 4):
-        l5[col + 2, 2 : 2 + n_rows // 4] = up_strip(l4, 2 + 2 * col, n_rows // 4)
-
-    lax.fori_loop(6, 8, near, 0)
-
-    for place, row in ((0, 9), (1, 0)):
-        ret_row[place] = acc[row, 1:9].astype(BF16)
-        ret_col[place] = acc[1:9, row].astype(BF16)
-        for other, col in ((0, 9), (1, 0)):
-            ret_cor[2 * place + other] = acc[row, col].astype(BF16)
-    halo_start(4)
-
-    cp_tr.wait()
-    for dx in range(-3, 4):
-        for dy in range(-1, 2):
-            for i in range(2):
-                for j in range(2):
-                    offset = (dx, 2 * dy + j - i)
-                    block = (
-                        tr_v[FAR.index(offset)] if offset in FAR else jnp.zeros((128, 128), BF16)
-                    )
-                    wt[
-                        3 * (dx + 3) + dy + 1,
-                        i * 128 : i * 128 + 128,
-                        j * 128 : j * 128 + 128,
-                    ] = block
-
-    halo_received(3)
-    halo_received(2)
-    halo_received(1)
+        l5[col + 2, 2 : 2 + n_rows // 4] = up_strip(l4, 2 + 2 * col, 2, n_rows // 4)
+
+    for number in (3, 2, 1):
+        halo_received(number, COL + CORNER)
 
     def sources(side, a, dx, dy):
         parts = []
@@ -457,6 +491,14 @@
 
             lax.fori_loop(0, 3, outer, 0)
             lax.fori_loop(0, 3, inner, 0)
+
+        if side == 0:
+            halo_received(4, ROW)
+            for place, row in ((0, 1), (1, 8)):
+                acc[row] += in_row[place].astype(F32)
+            for place, col in ((0, 9), (1, 0)):
+                ret_col[place] = acc[1:9, col].astype(BF16)
+            halo_start(4, COL)
 
     for a in range(2):
         for side in range(2):
@@ -492,12 +534,9 @@
                         for b in range(2):
                             lower[2 * u + a, 2 * v + b, side] = made[:, b * 128 : b * 128 + 128]
 
-    halo_received(4)
-    for place, row in ((0, 1), (1, 8)):
-        acc[row, 1:9] += in_row[place].astype(F32)
-        acc[1:9, row] += in_col[place].astype(F32)
-        for other, col in ((0, 1), (1, 8)):
-            acc[row, col] += in_cor[2 * place + other].astype(F32)
+    halo_received(4, COL)
+    for place, col in ((0, 1), (1, 8)):
+        acc[1:9, col] += in_col[place].astype(F32)
 
     def finish(x, carry):
         for y in range(8):
@@ -508,19 +547,20 @@
     lax.fori_loop(0, 8, finish, 0)
 
     for number in range(5):
-        halo_sent(number)
+        halo_sent(number, ROW + COL + (CORNER if number < 4 else []))
     for row, present in row_peers():
 
         @pl.when(present)
         def _():
             l3_row_copy(row, r).wait_send()
 
-    for j, col, present in col_peers():
-
-        @pl.when(present)
-        def _():
-            l3_col_copy(j, col).wait_send()
-
+    for step in range(5):
+
+        @pl.when(COL_SENDS[step])
+        def _():
+            l3_col_copy(step).wait_send()
+
+    l4_pass(c % 2).wait_send()
     for v, col, present in pair_peers():
 
         @pl.when(present)
@@ -553,12 +593,10 @@
         pltpu.VMEM((n_cols // 4 + 4, n_rows // 4 + 4) + box, BF16),
         pltpu.VMEM((8, 8, 32, 128), F32),
         pltpu.VMEM((10, 10, 32, 128), F32),
+        pltpu.VMEM((2, 10, 32, 128), BF16),
         pltpu.VMEM((2, 8, 32, 128), BF16),
+        pltpu.VMEM((2, 10, 32, 128), BF16),
         pltpu.VMEM((2, 8, 32, 128), BF16),
-        pltpu.VMEM((4, 32, 128), BF16),
-        pltpu.VMEM((2, 8, 32, 128), BF16),
-        pltpu.VMEM((2, 8, 32, 128), BF16),
-        pltpu.VMEM((4, 32, 128), BF16),
         pltpu.VMEM((21, 256, 256), BF16),
         pltpu.VMEM((2, 2, ROWS, 256), F32),
         pltpu.VMEM((2, 2) + box, BF16),
@@ -585,7 +623,7 @@
             kernel(n_rows, n_cols, *refs)
 
         result = jax.ShapeDtypeStruct(arrays[0].shape, BF16)
-        return pl.pallas_call(
+        made = pl.pallas_call(
             body,
             out_shape=(result, result),
             in_specs=[hbm, hbm, hbm, hbm, smem, hbm, hbm, hbm, hbm],
@@ -599,6 +637,40 @@
             ),
             name="fmm",
         )(*arrays)
+
+        def hand_on(pot_in, adj_in, pot_out, adj_out, held, in_sems, out_sems):
+            pairs = []
+            for which, (src, dst) in enumerate(((pot_in, pot_out), (adj_in, adj_out))):
+                for part in range(4):
+                    rows = pl.ds(2 * part, 2)
+                    slot = held.at[which, rows]
+                    pairs.append(
+                        (
+                            pltpu.make_async_copy(src.at[rows], slot, in_sems.at[which, part]),
+                            pltpu.make_async_copy(slot, dst.at[rows], out_sems.at[which, part]),
+                        )
+                    )
+            for fetch, _ in pairs:
+                fetch.start()
+            for fetch, store in pairs:
+                fetch.wait()
+                store.start()
+            for _, store in pairs:
+                store.wait()
+
+        return pl.pallas_call(
+            hand_on,
+            out_shape=(result, result),
+            in_specs=[hbm, hbm],
+            out_specs=(hbm, hbm),
+            scratch_shapes=[
+                pltpu.VMEM((2,) + arrays[0].shape, BF16),
+                pltpu.SemaphoreType.DMA((2, 4)),
+                pltpu.SemaphoreType.DMA((2, 4)),
+            ],
+            cost_estimate=pl.CostEstimate(flops=0, bytes_accessed=2097152, transcendentals=0),
+            name="hand_on",
+        )(*made)
 
     placed = (
         P("bx", "by", None, None),

time: 76 us -> 64.6 us (0.85)
  the two profiles are of different devices: /device:TPU:22 before, /device:TPU:29 now
where the time goes in v1:
time: 64.6 us; the launch traced here: 64.3 us
  Pallas kernels  63.7 us (99%)
    pallas_call x1, Pallas kernels, per_device(): pl.pallas_call(body, out_shape=(result, result), in_specs=[hbm, hbm, hbm,...  61.6 us
    pallas_call x1, Pallas kernels, per_device(): pl.pallas_call(hand_on, out_shape=(result, result), in_specs=[hbm, hbm],...  2.09 us

profile of v1, /device:TPU:29, one launch (start us, length us, event | category | flops | bytes accessed | tf_op | source)
XLA Modules:
  0.0 64.3 jit_solution(9646439672764650657)
XLA Ops:
  0.6 61.6 %fmm.1 = (bf16[8,8,32,128]{3,2,1,0:T(8,128)(2,1)}, bf16[8,8,32,128]{3,2,1,0:T(8,128)(2,1)}) custom-call(bf16[8,8,32,128]{3,2,1,0:T(8,128)(2,1)} %refs_0_.1, bf16[8,8,128]{2,1,0:T(8,128)(2,1)} %refs_1_.1, s32[8,8,128]{2,1,0:T(8,128)} %refs_2_.1, bf16[8,8,9,128,128]{4,3,2,1,0:T(8,128)(2,1)} %refs_3_.1, s32[8,8,9]{2,1,0:T(8,128)} %refs_4_.1, ...), custom_call_target="tpu_custom_call" | custom-call | flops 4300000256 | bytes 26000000 | tf_op jit(solution)/shard_map/fmm/pallas_call | solution.py:626
  62.2 2.1 %hand_on.1 = (bf16[8,8,32,128]{3,2,1,0:T(8,128)(2,1)}, bf16[8,8,32,128]{3,2,1,0:T(8,128)(2,1)}) custom-call(bf16[8,8,32,128]{3,2,1,0:T(8,128)(2,1)} %get-tuple-element.4.pot_in, bf16[8,8,32,128]{3,2,1,0:T(8,128)(2,1)} %get-tuple-element.5.adj_in), custom_call_target="tpu_custom_call" | custom-call | bytes 2097152 | tf_op jit(solution)/shard_map/hand_on/pallas_call | solution.py:661

commit v2 on v1

--- a/solution.py
+++ b/solution.py
@@ -37,7 +37,7 @@
     area_hbm,
     cond_hbm,
     nb_hbm,
-    mask_ref,
+    mask_hbm,
     sm_hbm,
     te_hbm,
     tr_hbm,
@@ -59,6 +59,7 @@
     l3,
     l4,
     l5,
+    mask_ref,
     nf,
     acc,
     ret_row,
@@ -94,6 +95,7 @@
     cp_area = pltpu.make_async_copy(area_hbm, area_v, in_sem.at[1])
     cp_cond = pltpu.make_async_copy(cond_hbm, cond_v, in_sem.at[2])
     cp_su = pltpu.make_async_copy(su_hbm, su_v, in_sem.at[3])
+    cp_mask = pltpu.make_async_copy(mask_hbm, mask_ref, in_sem.at[5])
     cp_tr = pltpu.make_async_copy(tr_hbm, tr_v, in_sem.at[4])
 
     def cp_sm(x):
@@ -112,9 +114,10 @@
         cp_sm(x).start()
         cp_te(x).start()
     cp_su.start()
+    cp_tr.start()
+    cp_mask.start()
     for x in range(8):
         cp_nb(x).start()
-    cp_tr.start()
 
     def clear(ref, rows, cols, width, wide):
         ref[0:width] = jnp.zeros((width,) + ref.shape[1:], ref.dtype)
@@ -256,16 +259,23 @@
 
     part = n_rows // 4
 
-    def l4_copy(v, col, owner):
-        rows = pl.ds(2 + part * (c % 2), part)
+    quarter = n_cols // 4
+    mirror = (c2 + quarter) % (2 * quarter)
+    ring = [quarter * (c2 // quarter) + (c2 + k) % quarter for k in range(1, quarter)]
+
+    def l4_copy(to, owner, slot):
+        place = l4.at[owner + 2, pl.ds(2 + part * (c % 2), part)]
         return pltpu.make_async_remote_copy(
-            src_ref=l4.at[owner + 2, rows],
-            dst_ref=l4.at[owner + 2, rows],
-            send_sem=s4_sem.at[v],
+            src_ref=place,
+            dst_ref=place,
+            send_sem=s4_sem.at[slot],
             recv_sem=r4_sem.at[owner],
-            device_id=(r, col),
+            device_id=(r, 2 * to + c % 2),
             device_id_type=MESH,
         )
+
+    def mirrored(v):
+        return (v + quarter) % (2 * quarter)
 
     def l4_pass(half):
         place = l4.at[pl.ds(2, n_cols // 2), pl.ds(2 + part * half, part)]
@@ -337,10 +347,12 @@
         def _():
             l3_row_copy(row, r).start()
 
+    for number in (1, 2, 3):
+        halo_start(number, ROW)
     halo_received(0, ROW)
     halo_start(0, CORNER)
-    for number in (3, 2, 1):
-        halo_start(number, ROW + COL)
+    for number in (3, 2):
+        halo_start(number, COL)
 
     cp_tr.wait()
     for dx in range(-3, 4):
@@ -358,6 +370,7 @@
                     ] = block
 
     halo_received(0, COL + CORNER)
+    cp_mask.wait()
 
     def near(x, carry):
         cp_nb(x).wait()
@@ -387,8 +400,6 @@
 
     for step in range(3):
         l3_col_start(step)
-    halo_received(3, ROW)
-    halo_start(3, CORNER)
 
     lax.fori_loop(2, 4, near, 0)
 
@@ -411,30 +422,23 @@
         return total.astype(BF16).reshape(rows, 2, 32, 128)
 
     l4[c2 + 2, pl.ds(2 + part * (c % 2), part)] = up_strip(l3, 2, 2 + 2 * part * (c % 2), part)
-    for v, col, present in pair_peers():
-
-        @pl.when(present)
-        def _():
-            l4_copy(v, col, c2).start()
-
+    l4_copy(mirror, c2, mirror).start()
+    for v in ring:
+        l4_copy(v, c2, v).start()
+
+    for number in (1,):
+        halo_start(number, COL)
+
+    lax.fori_loop(4, 6, near, 0)
+
+    l4_copy(mirror, mirror, mirror).wait_recv()
+    for v in ring:
+        l4_copy(v, mirror, mirrored(v)).start()
     l3_col_received(1)
     l3_col_start(3)
     l3_col_received(2)
     l3_col_start(4)
-    halo_received(2, ROW)
-    halo_start(2, CORNER)
-
-    lax.fori_loop(4, 6, near, 0)
-
-    halo_received(1, ROW)
-    halo_start(1, CORNER)
-    for v, col, present in pair_peers():
-
-        @pl.when(present)
-        def _():
-            l4_copy(v, col, jnp.int32(v)).wait_recv()
-
-    l4_pass(c % 2).start()
+    pass
 
     lax.fori_loop(6, 8, near, 0)
 
@@ -442,19 +446,18 @@
         ret_row[place] = acc[row].astype(BF16)
     halo_start(4, ROW)
 
-    l3_col_received(3)
-    l3_col_received(4)
-    l4_pass(1 - c % 2).wait_recv()
-    for col in range(n_cols // 4):
-        l5[col + 2, 2 : 2 + n_rows // 4] = up_strip(l4, 2 + 2 * col, 2, n_rows // 4)
-
-    for number in (3, 2, 1):
-        halo_received(number, COL + CORNER)
-
-    def sources(side, a, dx, dy):
+    halo_received(1, ROW)
+    halo_start(1, CORNER)
+    halo_received(1, COL)
+
+    INNER, OUTER, COARSE = (1, 2), (0, 3), ()
+
+    def sources(group, side, a, dx, dy):
         parts = []
-        for i in range(4):
+        for i in group:
             parts.append(leaf[2 * i + a + dx + 2, 1 + dy : 5 + dy, side].reshape(128, 256))
+        if group:
+            return jnp.concatenate(parts, axis=0)
         for i in range(2):
             parts.append(l1[2 * i + a + dx + 2, 1 + dy : 3 + dy, side].reshape(64, 256))
         parts.append(l2[a + dx + 2, 1 + dy, side])
@@ -468,37 +471,62 @@
             parts.append(jnp.concatenate([ref[col, row, side], ref[col + 1, row, side]], axis=1))
         return jnp.concatenate(parts, axis=0)
 
-    def interact(side, a, dx, columns):
-        taken = jnp.concatenate([sources(side, a, dx, dy) for dy in columns], axis=1)
-        if side == 0:
-            tiles = [wt[3 * (dx + 3) + dy + 1] for dy in columns]
-            return nt(taken, jnp.concatenate(tiles, axis=1))
-        tiles = [wt[3 * (3 - dx) + 1 - dy] for dy in columns]
-        return nn(taken, jnp.concatenate(tiles, axis=0))
-
+    def interact(group, side, a):
+        offsets = [
+            (dx, dy)
+            for dx in range(-2 - a, 4 - a)
+            for dy in (-1, 0, 1)
+            if abs(dx) >= 2 or dy != 0
+        ]
+        total = 0.0
+        for dx, dy in offsets:
+            taken = sources(group, side, a, dx, dy)
+            if side == 0:
+                total = total + nt(taken, wt[3 * (dx + 3) + dy + 1])
+            else:
+                total = total + nn(taken, wt[3 * (3 - dx) + 1 - dy])
+        return total
+
+    def inner_rows():
+        for side in range(2):
+            for a in range(2):
+                gain[side, a, 128:384] = interact(INNER, side, a)
+
+    inner_rows()
+    for v in ring:
+        l4_copy(v, v, v).wait_recv()
+        l4_copy(v, mirrored(v), mirrored(v)).wait_recv()
+
+    l4_pass(c % 2).start()
+    halo_received(2, ROW)
+    halo_start(2, CORNER)
+    halo_received(3, ROW)
+    halo_start(3, CORNER)
+    halo_received(4, ROW)
+    for place, row in ((0, 1), (1, 8)):
+        acc[row] += in_row[place].astype(F32)
+    for place, col in ((0, 9), (1, 0)):
+        ret_col[place] = acc[1:9, col].astype(BF16)
+    halo_start(4, COL)
+    halo_received(1, CORNER)
     for side in range(2):
         for a in range(2):
-            gain[side, a] = jnp.zeros((ROWS, 256), F32)
-
-            def outer(i, carry):
-                dx = i - 3 + 3 * (i // 2) if a == 1 else i + 1 - 3 * ((2 - i) // 2)
-                gain[side, a] += interact(side, a, dx, (-1, 0, 1))
-                return carry
-
-            def inner(i, carry):
-                gain[side, a] += interact(side, a, i - 1, (-1, 1))
-                return carry
-
-            lax.fori_loop(0, 3, outer, 0)
-            lax.fori_loop(0, 3, inner, 0)
-
-        if side == 0:
-            halo_received(4, ROW)
-            for place, row in ((0, 1), (1, 8)):
-                acc[row] += in_row[place].astype(F32)
-            for place, col in ((0, 9), (1, 0)):
-                ret_col[place] = acc[1:9, col].astype(BF16)
-            halo_start(4, COL)
+            made = interact(OUTER, side, a)
+            gain[side, a, 0:128] = made[0:128]
+            gain[side, a, 384:OFF1] = made[128:256]
+
+    pass
+    l3_col_received(3)
+    l3_col_received(4)
+    l4_pass(1 - c % 2).wait_recv()
+    for col in range(n_cols // 4):
+        l5[col + 2, 2 : 2 + n_rows // 4] = up_strip(l4, 2 + 2 * col, 2, n_rows // 4)
+    for number in (2, 3):
+        halo_received(number, COL + CORNER)
+
+    for side in range(2):
+        for a in range(2):
+            gain[side, a, OFF1:ROWS] = interact(COARSE, side, a)
 
     for a in range(2):
         for side in range(2):
@@ -561,18 +589,16 @@
             l3_col_copy(step).wait_send()
 
     l4_pass(c % 2).wait_send()
-    for v, col, present in pair_peers():
-
-        @pl.when(present)
-        def _():
-            l4_copy(v, col, c2).wait_send()
+    l4_copy(mirror, c2, mirror).wait_send()
+    for v in ring:
+        l4_copy(v, c2, v).wait_send()
+        l4_copy(v, mirror, mirrored(v)).wait_send()
 
 
 def solution(mesh):
     n_rows, n_cols = mesh.shape["bx"], mesh.shape["by"]
     hbm = pl.BlockSpec(memory_space=pl.ANY)
     vmem = pl.BlockSpec(memory_space=pltpu.VMEM)
-    smem = pl.BlockSpec(memory_space=pltpu.SMEM)
     box = (2, 32, 128)
     pair = (2, 32, 256)
     scratch = [
@@ -591,6 +617,7 @@
         pltpu.VMEM((6, n_rows + 4) + box, BF16),
         pltpu.VMEM((n_cols // 2 + 4, n_rows // 2 + 4) + box, BF16),
         pltpu.VMEM((n_cols // 4 + 4, n_rows // 4 + 4) + box, BF16),
+        pltpu.SMEM((8, 8, 9), jnp.int32),
         pltpu.VMEM((8, 8, 32, 128), F32),
         pltpu.VMEM((10, 10, 32, 128), F32),
         pltpu.VMEM((2, 10, 32, 128), BF16),
@@ -605,7 +632,7 @@
         pltpu.VMEM((2, 2) + box, BF16),
         pltpu.VMEM((4, 4) + box, BF16),
         pltpu.VMEM((8, 8) + box, BF16),
-        pltpu.SemaphoreType.DMA((5,)),
+        pltpu.SemaphoreType.DMA((6,)),
         pltpu.SemaphoreType.DMA((2, 8)),
         pltpu.SemaphoreType.DMA((8,)),
         pltpu.SemaphoreType.DMA((5, 8)),
@@ -622,11 +649,11 @@
         def body(*refs):
             kernel(n_rows, n_cols, *refs)
 
-        result = jax.ShapeDtypeStruct(arrays[0].shape, BF16)
-        made = pl.pallas_call(
+        kept = pltpu.VMEM(arrays[0].shape, BF16)
+        return pl.pallas_call(
             body,
-            out_shape=(result, result),
-            in_specs=[hbm, hbm, hbm, hbm, smem, hbm, hbm, hbm, hbm],
+            out_shape=(kept, kept),
+            in_specs=[hbm, hbm, hbm, hbm, hbm, hbm, hbm, hbm, hbm],
             out_specs=(vmem, vmem),
             scratch_shapes=scratch,
             compiler_params=pltpu.CompilerParams(
@@ -637,40 +664,6 @@
             ),
             name="fmm",
         )(*arrays)
-
-        def hand_on(pot_in, adj_in, pot_out, adj_out, held, in_sems, out_sems):
-            pairs = []
-            for which, (src, dst) in enumerate(((pot_in, pot_out), (adj_in, adj_out))):
-                for part in range(4):
-                    rows = pl.ds(2 * part, 2)
-                    slot = held.at[which, rows]
-                    pairs.append(
-                        (
-                            pltpu.make_async_copy(src.at[rows], slot, in_sems.at[which, part]),
-                            pltpu.make_async_copy(slot, dst.at[rows], out_sems.at[which, part]),
-                        )
-                    )
-            for fetch, _ in pairs:
-                fetch.start()
-            for fetch, store in pairs:
-                fetch.wait()
-                store.start()
-            for _, store in pairs:
-                store.wait()
-
-        return pl.pallas_call(
-            hand_on,
-            out_shape=(result, result),
-            in_specs=[hbm, hbm],
-            out_specs=(hbm, hbm),
-            scratch_shapes=[
-                pltpu.VMEM((2,) + arrays[0].shape, BF16),
-                pltpu.SemaphoreType.DMA((2, 4)),
-                pltpu.SemaphoreType.DMA((2, 4)),
-            ],
-            cost_estimate=pl.CostEstimate(flops=0, bytes_accessed=2097152, transcendentals=0),
-            name="hand_on",
-        )(*made)
 
     placed = (
         P("bx", "by", None, None),

time: 64.6 us -> 51.6 us (0.80)
  the two profiles are of different devices: /device:TPU:29 before, /device:TPU:22 now
where the time goes in v2:
time: 51.6 us; the launch traced here: 51.5 us
  Pallas kernels  49.3 us (96%)
  local copies, waits for them, and re-layouts  1.59 us (3%)
  between operations  0.64 us (1%)
    pallas_call x1, Pallas kernels, per_device(): pl.pallas_call(body, out_shape=(kept, kept), in_specs=[hbm, hbm, hbm, hbm...  49.3 us
    unnamed x2, local copies, waits for them, and re-layouts  1.59 us

profile of v2, /device:TPU:22, one launch (start us, length us, event | category | flops | bytes accessed | tf_op | source)
XLA Modules:
  0.0 51.5 jit_solution(3021093121630930191)
XLA Ops:
  0.6 49.3 %fmm.1 = (bf16[8,8,32,128]{3,2,1,0:T(8,128)(2,1)S(1)}, bf16[8,8,32,128]{3,2,1,0:T(8,128)(2,1)S(1)}) custom-call(bf16[8,8,32,128]{3,2,1,0:T(8,128)(2,1)} %refs_0_.1, bf16[8,8,128]{2,1,0:T(8,128)(2,1)} %refs_1_.1, s32[8,8,128]{2,1,0:T(8,128)} %refs_2_.1, bf16[8,8,9,128,128]{4,3,2,1,0:T(8,128)(2,1)} %refs_3_.1, s32[8,8,9]{2,1,0:T(8,128)} %refs_4_.1, ...), custom_call_target="tpu_custom_call" | custom-call | flops 4300000256 | bytes 26000000 | tf_op jit(solution)/shard_map/fmm/pallas_call | solution.py:653
  49.9 0.8 %copy.13 = bf16[8,8,32,128]{3,2,1,0:T(8,128)(2,1)} copy(bf16[8,8,32,128]{3,2,1,0:T(8,128)(2,1)S(1)} %get-tuple-element.2) | data formatting | bytes 1048576
  50.7 0.8 %copy.14 = bf16[8,8,32,128]{3,2,1,0:T(8,128)(2,1)} copy(bf16[8,8,32,128]{3,2,1,0:T(8,128)(2,1)S(1)} %get-tuple-element.3) | data formatting | bytes 1048576

commit v3 on v2

--- a/solution.py
+++ b/solution.py
@@ -175,8 +175,16 @@
             )[number]
             src_rows, dst_rows = edge(dx, rows, width)
             src_cols, dst_cols = edge(dy, cols, wide)
-            src = ref.at[src_rows if dy == 0 or dx == 0 else dst_rows, src_cols]
-            dst = ref.at[dst_rows, dst_cols]
+            if number < 2 or dx * dy != 0:
+                src = ref.at[src_rows if dy == 0 or dx == 0 else dst_rows, src_cols]
+                dst = ref.at[dst_rows, dst_cols]
+            elif dy == 0:
+                src = ref.at[rows if dx > 0 else 3, 1 : cols + 1]
+                dst = ref.at[0 if dx > 0 else rows + 3, 1 : cols + 1]
+            else:
+                lanes = slice(0, 128) if dy > 0 else slice(128, 256)
+                src = ref.at[src_rows, cols if dy > 0 else 1, :, :, lanes]
+                dst = ref.at[dst_rows, 0 if dy > 0 else cols + 1, :, :, lanes]
         return pltpu.make_async_remote_copy(
             src_ref=src,
             dst_ref=dst,
@@ -325,6 +333,41 @@
     cp_su.wait()
     ups = [jnp.concatenate([su_v[a, 0], su_v[a, 1]], axis=1) for a in range(2)]
 
+    def ring_rows(lower, upper, rows, cols):
+        total = sum(
+            nt(
+                jnp.concatenate(
+                    [lower[low + a, 1 : cols + 1].reshape(cols * 64, 256) for low in (0, 2 * rows + 2)],
+                    axis=0,
+                ),
+                ups[a],
+            )
+            for a in range(2)
+        )
+        made = total.astype(BF16).reshape(2, cols, 2, 32, 128)
+        for place, row in ((0, 1), (1, rows + 2)):
+            for v in range(cols):
+                upper[row, 1 + v // 2, :, :, (v % 2) * 128 : (v % 2) * 128 + 128] = made[place, v]
+
+    def ring_cols(lower, upper, rows, cols):
+        total = sum(
+            nt(
+                jnp.concatenate(
+                    [
+                        lower[2 * u + a + 2, col].reshape(64, 256)
+                        for col in (0, cols + 1)
+                        for u in range(rows)
+                    ],
+                    axis=0,
+                ),
+                ups[a],
+            )
+            for a in range(2)
+        )
+        made = total.astype(BF16).reshape(2, rows, 2, 32, 128)
+        upper[2 : rows + 2, 0, :, :, 128:256] = made[0]
+        upper[2 : rows + 2, cols // 2 + 1, :, :, 0:128] = made[1]
+
     for u in range(4):
         total = sum(nt(leaf[2 * u + a + 2, 1:5].reshape(256, 256), ups[a]) for a in range(2))
         made = total.astype(BF16).reshape(4, 2, 32, 128)
@@ -351,7 +394,7 @@
         halo_start(number, ROW)
     halo_received(0, ROW)
     halo_start(0, CORNER)
-    for number in (3, 2):
+    for number in (1,):
         halo_start(number, COL)
 
     cp_tr.wait()
@@ -426,10 +469,10 @@
     for v in ring:
         l4_copy(v, c2, v).start()
 
-    for number in (1,):
+    for number in (2, 3):
         halo_start(number, COL)
 
-    lax.fori_loop(4, 6, near, 0)
+    lax.fori_loop(4, 7, near, 0)
 
     l4_copy(mirror, mirror, mirror).wait_recv()
     for v in ring:
@@ -438,9 +481,8 @@
     l3_col_start(3)
     l3_col_received(2)
     l3_col_start(4)
-    pass
-
-    lax.fori_loop(6, 8, near, 0)
+
+    lax.fori_loop(7, 8, near, 0)
 
     for place, row in ((0, 9), (1, 0)):
         ret_row[place] = acc[row].astype(BF16)
@@ -448,6 +490,7 @@
 
     halo_received(1, ROW)
     halo_start(1, CORNER)
+    ring_rows(leaf, l1, 4, 4)
     halo_received(1, COL)
 
     INNER, OUTER, COARSE = (1, 2), (0, 3), ()
@@ -500,29 +543,31 @@
     l4_pass(c % 2).start()
     halo_received(2, ROW)
     halo_start(2, CORNER)
+    ring_rows(l1, l2, 2, 2)
     halo_received(3, ROW)
     halo_start(3, CORNER)
+    halo_received(1, CORNER)
+    for side in range(2):
+        for a in range(2):
+            made = interact(OUTER, side, a)
+            gain[side, a, 0:128] = made[0:128]
+            gain[side, a, 384:OFF1] = made[128:256]
+
     halo_received(4, ROW)
     for place, row in ((0, 1), (1, 8)):
         acc[row] += in_row[place].astype(F32)
     for place, col in ((0, 9), (1, 0)):
         ret_col[place] = acc[1:9, col].astype(BF16)
     halo_start(4, COL)
-    halo_received(1, CORNER)
-    for side in range(2):
-        for a in range(2):
-            made = interact(OUTER, side, a)
-            gain[side, a, 0:128] = made[0:128]
-            gain[side, a, 384:OFF1] = made[128:256]
-
-    pass
     l3_col_received(3)
     l3_col_received(4)
     l4_pass(1 - c % 2).wait_recv()
     for col in range(n_cols // 4):
         l5[col + 2, 2 : 2 + n_rows // 4] = up_strip(l4, 2 + 2 * col, 2, n_rows // 4)
-    for number in (2, 3):
-        halo_received(number, COL + CORNER)
+    halo_received(2, COL + CORNER)
+    ring_cols(leaf, l1, 4, 4)
+    ring_cols(l1, l2, 2, 2)
+    halo_received(3, COL + CORNER)
 
     for side in range(2):
         for a in range(2):

time: 51.6 us -> 47.2 us (0.915)
  the two profiles are of different devices: /device:TPU:22 before, /device:TPU:97 now
where the time goes in v3:
time: 47.2 us; the launch traced here: 47.1 us
  Pallas kernels  44.8 us (95%)
  local copies, waits for them, and re-layouts  1.59 us (3%)
  between operations  0.64 us (1%)
    pallas_call x1, Pallas kernels, per_device(): pl.pallas_call(body, out_shape=(kept, kept), in_specs=[hbm, hbm, hbm, hbm...  44.8 us
    unnamed x2, local copies, waits for them, and re-layouts  1.59 us

profile of v3, /device:TPU:97, one launch (start us, length us, event | category | flops | bytes accessed | tf_op | source)
XLA Modules:
  0.0 47.1 jit_solution(10240751394833811437)
XLA Ops:
  0.6 44.8 %fmm.1 = (bf16[8,8,32,128]{3,2,1,0:T(8,128)(2,1)S(1)}, bf16[8,8,32,128]{3,2,1,0:T(8,128)(2,1)S(1)}) custom-call(bf16[8,8,32,128]{3,2,1,0:T(8,128)(2,1)} %refs_0_.1, bf16[8,8,128]{2,1,0:T(8,128)(2,1)} %refs_1_.1, s32[8,8,128]{2,1,0:T(8,128)} %refs_2_.1, bf16[8,8,9,128,128]{4,3,2,1,0:T(8,128)(2,1)} %refs_3_.1, s32[8,8,9]{2,1,0:T(8,128)} %refs_4_.1, ...), custom_call_target="tpu_custom_call" | custom-call | flops 4300000256 | bytes 26000000 | tf_op jit(solution)/shard_map/fmm/pallas_call | solution.py:698
  45.5 0.8 %copy.13 = bf16[8,8,32,128]{3,2,1,0:T(8,128)(2,1)} copy(bf16[8,8,32,128]{3,2,1,0:T(8,128)(2,1)S(1)} %get-tuple-element.2) | data formatting | bytes 1048576
  46.3 0.8 %copy.14 = bf16[8,8,32,128]{3,2,1,0:T(8,128)(2,1)} copy(bf16[8,8,32,128]{3,2,1,0:T(8,128)(2,1)S(1)} %get-tuple-element.3) | data formatting | bytes 1048576

commit v4 on v3

--- a/solution.py
+++ b/solution.py
@@ -491,6 +491,11 @@
     halo_received(1, ROW)
     halo_start(1, CORNER)
     ring_rows(leaf, l1, 4, 4)
+    halo_received(2, ROW)
+    halo_start(2, CORNER)
+    ring_rows(l1, l2, 2, 2)
+    halo_received(3, ROW)
+    halo_start(3, CORNER)
     halo_received(1, COL)
 
     INNER, OUTER, COARSE = (1, 2), (0, 3), ()
@@ -541,11 +546,6 @@
         l4_copy(v, mirrored(v), mirrored(v)).wait_recv()
 
     l4_pass(c % 2).start()
-    halo_received(2, ROW)
-    halo_start(2, CORNER)
-    ring_rows(l1, l2, 2, 2)
-    halo_received(3, ROW)
-    halo_start(3, CORNER)
     halo_received(1, CORNER)
     for side in range(2):
         for a in range(2):

time: 47.2 us -> 46.2 us (0.979)
  the two profiles are of different devices: /device:TPU:97 before, /device:TPU:22 now
where the time goes in v4:
time: 46.2 us; the launch traced here: 45.7 us
  Pallas kernels  43.4 us (94%)
  local copies, waits for them, and re-layouts  1.59 us (3%)
  between operations  0.64 us (1%)
    pallas_call x1, Pallas kernels, per_device(): pl.pallas_call(body, out_shape=(kept, kept), in_specs=[hbm, hbm, hbm, hbm...  43.4 us
    unnamed x2, local copies, waits for them, and re-layouts  1.59 us

profile of v4, /device:TPU:22, one launch (start us, length us, event | category | flops | bytes accessed | tf_op | source)
XLA Modules:
  0.0 45.7 jit_solution(9879740286964033044)
XLA Ops:
  0.6 43.4 %fmm.1 = (bf16[8,8,32,128]{3,2,1,0:T(8,128)(2,1)S(1)}, bf16[8,8,32,128]{3,2,1,0:T(8,128)(2,1)S(1)}) custom-call(bf16[8,8,32,128]{3,2,1,0:T(8,128)(2,1)} %refs_0_.1, bf16[8,8,128]{2,1,0:T(8,128)(2,1)} %refs_1_.1, s32[8,8,128]{2,1,0:T(8,128)} %refs_2_.1, bf16[8,8,9,128,128]{4,3,2,1,0:T(8,128)(2,1)} %refs_3_.1, s32[8,8,9]{2,1,0:T(8,128)} %refs_4_.1, ...), custom_call_target="tpu_custom_call" | custom-call | flops 4300000256 | bytes 26000000 | tf_op jit(solution)/shard_map/fmm/pallas_call | solution.py:698
  44.1 0.8 %copy.13 = bf16[8,8,32,128]{3,2,1,0:T(8,128)(2,1)} copy(bf16[8,8,32,128]{3,2,1,0:T(8,128)(2,1)S(1)} %get-tuple-element.2) | data formatting | bytes 1048576
  44.9 0.8 %copy.14 = bf16[8,8,32,128]{3,2,1,0:T(8,128)(2,1)} copy(bf16[8,8,32,128]{3,2,1,0:T(8,128)(2,1)S(1)} %get-tuple-element.3) | data formatting | bytes 1048576
